TPU v7x, 128 devices: a whole 4x4x4 slice. The times are simulated.
128 devices in a mesh: dp: 32 (over z, y, core), mp: 4 (over x).
Axes of the slice: x: 4, y: 4, z: 4, core: 2. Of those that a mesh axis runs over, the one named last changes fastest.
Arguments:
- patches: bfloat16 [49152, 128], P(('dp', 'mp')), may hold values from -6 to 6
- row_count: int32 [128], P(('dp', 'mp')), may hold values from 0 to 384, as said below
- target_group: int32 [49152], P(('dp', 'mp')), may hold values from 0 to 31, as said below
- target_offset: int32 [49152], P(('dp', 'mp')), may hold values from 0 to 639, as said below
- embed: bfloat16 [128, 6144], replicated, may hold values from -0.5 to 0.5
- norm_gain: bfloat16 [6144], replicated, may hold values from 0.099609375 to 1.8984375
- readout: bfloat16 [6144, 128], P('mp'), may hold values from -0.078125 to 0.078125
- target: bfloat16 [20480, 128], P('dp'), may hold values from -12 to 12
- master: float32 [6144, 6144], P('dp', 'mp'), may hold values from -6 to 6
- moment1: float32 [6144, 6144], P('dp', 'mp'), may hold values from -2 to 2
- moment2: float32 [6144, 6144], P('dp', 'mp'), may hold values from 0.0034722222 to 0.1388889
Outputs:
- prediction: float32 [20480, 128], P('dp')
- master_new: float32 [6144, 6144], P('dp', 'mp')
- moment1_new: float32 [6144, 6144], P('dp', 'mp')
- moment2_new: float32 [6144, 6144], P('dp', 'mp')
- weight_copy: bfloat16 [6144, 6144], P('dp', 'mp')
Inputs may be any that keep to these rules, and one draw needn't show every extreme that they name: Device i holds its live patch rows in its first row_count[i] slots; some device holds 384 of them in every draw. Over the live slots of all devices, each pair (target_group, target_offset) of the 20480 positions occurs exactly once; values in slots past row_count are arbitrary within the range. Call target_offset // 160 the block of a row. Each (batch, block) receives exactly 160 live rows; one device sends at most 3 live rows to one (batch, block), and every (batch, block) gets 3 rows from some device.
All inputs are finite; a program needn't handle non-finite values.
Results may differ from a plain program's by a relative error of at most 0.03.
Values may be sent and summed in bfloat16 or wider, within the bound.
A program may use at most 128 MiB of HBM per device.

v0:
```python
import jax
import jax.numpy as jnp
from jax import lax
from jax.experimental import pallas as pl
from jax.experimental.pallas import tpu as pltpu
from jax.sharding import PartitionSpec as P

gelu_const = 0.7978845608028654
cubic = 0.044715
beta_one = 0.9
beta_two = 0.95
learn_rate = 0.01
decay_rate = 0.1
adam_epsilon = 1e-08
step_count = 20

WIDTH = 6144
ROWS = 192
COLS = 768
TOKENS = 1280
BLOCK = 160
SLOTS = 384
SCALE = 1.0 / WIDTH**0.5
MESH = pl.DeviceIdType.MESH
f32, bf16, i32 = jnp.float32, jnp.bfloat16, jnp.int32

NN = (((1,), (0,)), ((), ()))
NT = (((1,), (1,)), ((), ()))
TN = (((0,), (0,)), ((), ()))


def matmul(a, b, dims=NN):
    return lax.dot_general(a, b, dims, preferred_element_type=f32)


def iota(shape, axis):
    return lax.broadcasted_iota(i32, shape, axis)


def kernel(
    row_count,
    patches,
    group_row,
    offset_row,
    gain,
    embed_hbm,
    readout_hbm,
    target_hbm,
    master_hbm,
    pred_out,
    grad_out,
    emb,
    ro,
    tgt,
    master_own,
    master_far,
    far_half,
    w,
    hg,
    acc,
    delta,
    ssq,
    gain_rows,
    perm,
    out1,
    in1,
    out2,
    in2,
    batch,
    part_out,
    part_in,
    part_own,
    err_own,
    err_in,
    core_in,
    zhalf_in,
    zfull_in,
    y_in,
    pair_in,
    local_sem,
    r1_send,
    r1_recv,
    r2_send,
    r2_recv,
    r3_send,
    r3_recv,
    ag_send,
    ag_recv,
    part_send,
    part_recv,
    err_send,
    err_recv,
    rs_send,
    rs_recv,
):
    dp, x = lax.axis_index("dp"), lax.axis_index("mp")
    z = lax.div(dp, 8)
    y = lax.rem(lax.div(dp, 2), 4)
    c = lax.rem(dp, 2)
    k = lax.div(y, 2)
    p = lax.rem(y, 2)
    half = lax.rem(p + k, 2)
    yp = y + 1 - 2 * p
    ya = 3 - y
    yap = 3 - yp
    kk, oc = 1 - k, 1 - c
    zp, zm, z2 = lax.rem(z + 1, 4), lax.rem(z + 3, 4), lax.rem(z + 2, 4)
    member = z * 4 + k * 2 + c
    sub = p * 4 + x
    zs = (z, zp, zm, z2)
    ys = (y, yp, ya, yap)

    def device(zz, yy, cc, xx):
        return ((zz * 4 + yy) * 2 + cc, xx)

    def member_device(i):
        other = lax.rem(member + i, 16)
        zz, kz, cc = lax.div(other, 4), lax.rem(lax.div(other, 2), 2), lax.rem(other, 2)
        return other, device(zz, 2 * kz + p, cc, x)

    def sub_device(i):
        other = lax.rem(sub + i, 8)
        return other, device(z, 2 * k + lax.div(other, 4), c, lax.rem(other, 4))

    def remote(src, dst, send, recv, to):
        return pltpu.make_async_remote_copy(
            src_ref=src, dst_ref=dst, send_sem=send, recv_sem=recv, device_id=to, device_id_type=MESH
        )

    def chunk(zz, yy, cc, low=0, count=ROWS):
        start = pl.multiple_of(lax.rem(yy, 2) * (2 * ROWS) + cc * ROWS + low, 32)
        return w.at[zz * 2 + lax.div(yy, 2), pl.ds(start, count), :]

    def span(index, size, count=None):
        return pl.ds(pl.multiple_of(index * size, size), size if count is None else count)

    barrier = pltpu.get_barrier_semaphore()
    peers = [member_device(i)[1] for i in range(1, 16)]
    peers += [sub_device(i)[1] for i in range(1, 8)]
    peers += [device(z, ya, c, x)]
    for peer in peers:
        pl.semaphore_signal(barrier, inc=1, device_id=peer, device_id_type=MESH)

    loads = [
        (master_hbm.at[:, span(half, COLS)], master_own),
        (master_hbm.at[:, span(1 - half, COLS)], master_far),
        (embed_hbm, emb),
        (readout_hbm.at[span(half, COLS), :], ro),
        (target_hbm, tgt),
    ]
    loads = [pltpu.make_async_copy(a, b, local_sem.at[i]) for i, (a, b) in enumerate(loads)]
    for load in loads:
        load.start()

    def as_row(ref):
        return jnp.concatenate([ref[i : i + 1, :] for i in range(SLOTS // 128)], axis=1)

    group, offset = as_row(group_row), as_row(offset_row)
    live = iota((1, SLOTS), 1) < row_count[0]
    to_member = (group >> 3) * 4 + ((group >> 2) & 1) * 2 + (group & 1)
    block = sum((offset >= BLOCK * i).astype(i32) for i in range(1, 4))
    place = offset - block * BLOCK + 1
    to_sub = ((group >> 1) & 1) * 4 + block
    key = jnp.where(live, to_member * 8 + to_sub, -1)
    row_id, col_id = iota((SLOTS, SLOTS), 0), iota((SLOTS, SLOTS), 1)

    def column(values):
        wide = jnp.broadcast_to(values.astype(f32), (SLOTS, SLOTS))
        return jnp.sum(jnp.where(row_id == col_id, wide, 0.0), axis=1, keepdims=True)

    same = (column(key) == key.astype(f32)) & (row_id < col_id)
    rank = jnp.sum(jnp.where(same, 1.0, 0.0), axis=0, keepdims=True).astype(i32)
    slot = jnp.where(live, to_member * 32 + rank * 8 + to_sub, -1)
    pick = jnp.where(iota((512, SLOTS), 0) == slot, 1.0, 0.0).astype(bf16)
    marks = jnp.broadcast_to(column(place), (SLOTS, 128)).astype(bf16)
    out1[:, :128] = matmul(pick, patches[...]).astype(bf16)
    out1[:, 128:] = matmul(pick, marks).astype(bf16)

    loads[0].wait()
    loads[1].wait()
    own = chunk(z, y, c)
    own[...] = master_own[...].astype(bf16)
    far_half[...] = master_far[...].astype(bf16)

    pl.semaphore_wait(barrier, len(peers))

    sends = []

    def launch(copy):
        copy.start()
        sends.append(copy)

    for i in range(1, 16):
        other, to = member_device(i)
        launch(
            remote(
                out1.at[span(other, 32), :],
                in1.at[span(member, 32), :],
                r1_send.at[other],
                r1_recv.at[member],
                to,
            )
        )

    def gather(event, src, dst, to):
        remote(src, dst, ag_send.at[event], ag_recv.at[event], to).start()

    def gathered(event, dst):
        remote(dst, dst, ag_send.at[event], ag_recv.at[event], device(z, y, oc, x)).wait_recv()

    def along_z(event, zz, yy, low=0, count=ROWS, up=True):
        piece = chunk(zz, yy, c, low, count)
        gather(event, piece, piece, device(zp if up else zm, y, c, x))

    def full_z(event, yy):
        along_z(event, z, yy)
        along_z(event + 1, z, yy, up=False)

    def halves_z(event, yy):
        along_z(event + 2, zm, yy, 0, ROWS // 2)
        along_z(event + 3, zp, yy, ROWS // 2, ROWS // 2, up=False)

    def wait_full(event, yy):
        gathered(event, chunk(zm, yy, c))
        gathered(event + 1, chunk(zp, yy, c))

    def wait_halves(event, yy):
        gathered(event + 2, chunk(z2, yy, c, 0, ROWS // 2))
        gathered(event + 3, chunk(z2, yy, c, ROWS // 2, ROWS // 2))

    def along_y(j):
        piece = chunk(zs[j], yp, c)
        gather(14 + j, piece, piece, device(z, ya, c, x))

    def wait_y(j):
        gathered(14 + j, chunk(zs[j], yap, c))

    def relay(j, l):
        piece = chunk(zs[j], ys[l], c)
        gather(18 + j * 4 + l, piece, piece, device(z, y, oc, x))

    def wait_relay(j, l):
        gathered(18 + j * 4 + l, chunk(zs[j], ys[l], oc))

    gather(0, far_half, own, device(z, yp, c, x))
    gather(1, own, own, device(z, ya, c, x))
    full_z(2, y)
    relay(0, 0)

    gains = gain[...].astype(f32)
    lanes = COLS // 128
    for j in range(8):
        rows = [gains[lanes * j + l : lanes * j + l + 1] for l in range(lanes)]
        gain_rows[j] = jnp.concatenate(rows, axis=1)
    ssq[...] = jnp.zeros_like(ssq)
    acc[...] = jnp.zeros_like(acc)
    in1[span(member, 32), :] = out1[span(member, 32), :]
    row512 = iota((512, 512), 0)
    source = (row512 & 15) * 32 + ((row512 >> 4) & 3) * 8 + (row512 >> 6)
    perm[...] = jnp.where(iota((512, 512), 1) == source, 1.0, 0.0).astype(bf16)
    for i in range(1, 16):
        other, to = member_device(i)
        landed = in1.at[span(other, 32), :]
        remote(landed, landed, r1_send.at[other], r1_recv.at[other], to).wait_recv()
    out2[...] = matmul(perm[...], in1[...]).astype(bf16)
    for i in range(1, 8):
        other, to = sub_device(i)
        launch(
            remote(
                out2.at[span(other, 64, 48), :],
                in2.at[span(sub, 48), :],
                r2_send.at[other],
                r2_recv.at[sub],
                to,
            )
        )
    in2[span(sub, 48), :] = out2[span(sub, 64, 48), :]

    gathered(0, chunk(z, yp, c))
    full_z(10, yp)
    along_y(0)
    relay(0, 1)

    for i in range(1, 8):
        other, to = sub_device(i)
        landed = in2.at[span(other, 48), :]
        remote(landed, landed, r2_send.at[other], r2_recv.at[other], to).wait_recv()
    mark = in2[:, 128:].astype(f32)
    lane = iota((SLOTS, 128), 1)
    to_place = jnp.concatenate(
        [
            jnp.where(mark == (lane + 1).astype(f32), 1.0, 0.0),
            jnp.where(mark == (lane + 129).astype(f32), 1.0, 0.0),
        ],
        axis=1,
    ).astype(bf16)
    mine = span(sub, BLOCK)
    batch[mine, :] = matmul(to_place, in2[:, :128], TN)[:BLOCK].astype(bf16)
    for i in range(1, 8):
        other, to = sub_device(i)
        launch(remote(batch.at[mine, :], batch.at[mine, :], r3_send.at[other], r3_recv.at[sub], to))

    wait_full(2, y)
    relay(1, 0)
    relay(2, 0)
    gathered(1, chunk(z, ya, c))
    relay(0, 2)
    wait_full(10, yp)
    along_y(1)
    along_y(2)
    halves_z(10, yp)
    full_z(6, ya)
    relay(1, 1)
    relay(2, 1)

    for i in range(1, 8):
        other, to = sub_device(i)
        landed = batch.at[span(other, BLOCK), :]
        remote(landed, landed, r3_send.at[other], r3_recv.at[other], to).wait_recv()
    loads[2].wait()

    def embed(j, carry):
        @pl.when(j == 3)
        def _():
            wait_halves(10, yp)
            halves_z(2, y)
            relay(3, 1)
            wait_y(0)
            relay(0, 3)

        @pl.when(j == 6)
        def _():
            wait_full(6, ya)
            halves_z(6, ya)
            relay(1, 2)
            relay(2, 2)

        v = matmul(batch[...], emb[:, span(j, COLS)])
        t = jnp.tanh(v * (gelu_const + (gelu_const * cubic) * (v * v)))
        twice = v + v * t
        square = twice * twice
        total = sum(square[:, l * 128 : (l + 1) * 128] for l in range(COLS // 128))
        ssq[...] += total
        hg[j] = (twice * gain_rows[j]).astype(bf16)
        return carry

    lax.fori_loop(0, 8, embed, 0)

    def forward(i, carry):
        @pl.when(i == 0)
        def _():
            for l in range(2):
                wait_relay(0, l)

        @pl.when(i == 1)
        def _():
            for l in range(2, 4):
                wait_relay(0, l)

        @pl.when(i == 2)
        def _():
            for l in range(2):
                wait_relay(1, l)

        @pl.when(i == 3)
        def _():
            wait_y(1)
            along_y(3)
            relay(1, 3)
            wait_halves(2, y)
            relay(3, 0)
            for l in range(2, 4):
                wait_relay(1, l)

        @pl.when(i == 4)
        def _():
            wait_y(2)
            relay(2, 3)
            for l in range(2):
                wait_relay(2, l)

        @pl.when(i == 5)
        def _():
            wait_halves(6, ya)
            relay(3, 2)
            for l in range(2, 4):
                wait_relay(2, l)

        @pl.when(i == 6)
        def _():
            for l in range(2):
                wait_relay(3, l)

        @pl.when(i == 7)
        def _():
            wait_y(3)
            relay(3, 3)
            for l in range(2, 4):
                wait_relay(3, l)

        j, far = lax.div(i, 2), lax.rem(i, 2)
        zz = lax.rem(z + j + lax.div(j, 2) - 2 * lax.div(j, 3), 4)
        g = zz * 2 + k + far * (1 - 2 * k)
        acc[...] += matmul(hg[g], w[g])
        return carry

    lax.fori_loop(0, 8, forward, 0)

    loads[3].wait()
    loads[4].wait()

    def row_scale(rows):
        mean4 = jnp.sum(ssq[rows, :], axis=1, keepdims=True) * (0.25 / WIDTH)
        return lax.rsqrt(mean4 + 1e-05) * (0.5 * SCALE)

    def partial(index):
        rows = span(index, BLOCK)
        v = acc[rows, :] * row_scale(rows)
        t = jnp.tanh(v * (gelu_const + (gelu_const * cubic) * (v * v)))
        return matmul((0.5 * v * (1.0 + t)).astype(bf16), ro[...])

    for i in range(1, 8):
        other, to = sub_device(i)
        part_out[other] = partial(other).astype(bf16)
        launch(
            remote(part_out.at[other], part_in.at[sub], part_send.at[other], part_recv.at[sub], to)
        )
    part_own[...] = partial(sub)

    def slope(i, carry):
        rows = span(i, BLOCK)
        r = row_scale(rows)
        v = acc[rows, :] * r
        t = jnp.tanh(v * (gelu_const + (gelu_const * cubic) * (v * v)))
        acc[rows, :] = r * (
            0.5 * (1.0 + t)
            + (0.5 * gelu_const) * v * (1.0 - t * t) * (1.0 + (3.0 * cubic) * (v * v))
        )
        return carry

    lax.fori_loop(0, 8, slope, 0)
    total = part_own[...]
    for i in range(1, 8):
        other, to = sub_device(i)
        landed = part_in.at[other]
        remote(landed, landed, part_send.at[other], part_recv.at[other], to).wait_recv()
        total = total + part_in[other].astype(f32)
    total = total.astype(bf16)
    err_in[sub] = total
    err_own[...] = (total.astype(f32) - tgt[span(x, BLOCK), :].astype(f32)).astype(bf16)
    for i in range(4):
        other = lax.rem(x + i, 4)
        launch(
            remote(
                err_own,
                err_in.at[sub],
                err_send.at[(1 - p) * 4 + other],
                err_recv.at[sub],
                device(z, yp, c, other),
            )
        )
        if i:
            launch(
                remote(
                    err_in.at[sub],
                    err_in.at[sub],
                    err_send.at[p * 4 + other],
                    err_recv.at[sub],
                    device(z, y, c, other),
                )
            )

    def backward(index, errors):
        rows = span(index, BLOCK)
        delta[rows, :] = (matmul(errors, ro[...], NT) * acc[rows, :]).astype(bf16)

    for i in range(4):
        other = lax.rem(x + i, 4)
        index = p * 4 + other
        landed = err_in.at[index]
        if i:
            to = device(z, y, c, other)
            remote(landed, landed, err_send.at[index], err_recv.at[index], to).wait_recv()
        rows = span(other, BLOCK)
        pred_out[rows, :] = err_in[index]
        backward(index, (err_in[index].astype(f32) - tgt[rows, :].astype(f32)).astype(bf16))
    for i in range(4):
        other = lax.rem(x + i, 4)
        index = (1 - p) * 4 + other
        landed = err_in.at[index]
        to = device(z, yp, c, other)
        remote(landed, landed, err_send.at[index], err_recv.at[index], to).wait_recv()
        backward(index, err_in[index])

    for event in range(34):
        piece = far_half.at[: ROWS // 2, :] if event in (4, 5, 8, 9, 12, 13) else far_half
        to = device(z, y, oc, x)
        remote(piece, piece, ag_send.at[event], ag_recv.at[event], to).wait_send()

    def scatter(event, src, dst, to):
        launch(remote(src, dst, rs_send.at[event], rs_recv.at[event], to))

    def scattered(event, dst):
        remote(dst, dst, rs_send.at[event], rs_recv.at[event], device(z, y, oc, x)).wait_recv()

    def add(target, terms, count=ROWS):
        def tile(i, carry):
            rows = span(i, 48)
            value = target[rows, :].astype(f32)
            for term in terms:
                value = value + term[rows, :].astype(f32)
            target[rows, :] = value.astype(bf16)
            return carry

        lax.fori_loop(0, count // 48, tile, 0)

    def core_slot(zz, yy):
        start = pl.multiple_of(lax.rem(yy, 2) * ROWS, 32)
        return core_in.at[zz * 2 + lax.div(yy, 2), pl.ds(start, ROWS), :]

    def gradient(j, far):
        zz = zs[j]
        g = zz * 2 + (kk if far else k)


        def tile(i, carry):
            rows = span(i, 384)
            w[g, rows, :] = matmul(hg[g, :, rows], delta[...], TN).astype(bf16)
            return carry

        lax.fori_loop(0, 2, tile, 0)
        for l in (3, 2) if far else (0, 1):
            scatter(j * 4 + l, chunk(zz, ys[l], oc), core_slot(zz, ys[l]), device(z, y, oc, x))

    def cores(j, l):
        scattered(j * 4 + l, core_slot(zs[j], ys[l]))
        add(chunk(zs[j], ys[l], c), [core_slot(zs[j], ys[l])])

    kinds = {0: y, 1: ya, 2: yp}
    down, up = device(zm, y, c, x), device(zp, y, c, x)

    def send_halves(kind):
        yy = kinds[kind]
        event = 16 + 4 * kind
        scatter(event, chunk(z2, yy, c, 0, ROWS // 2), zhalf_in.at[kind, 0], down)
        scatter(event + 1, chunk(z2, yy, c, ROWS // 2, ROWS // 2), zhalf_in.at[kind, 1], up)

    def send_full(kind, side):
        yy = kinds[kind]
        event = 16 + 4 * kind + side
        zz = (zm, zp)[side]
        scattered(event, zhalf_in.at[kind, side])
        add(
            chunk(zz, yy, c, side * (ROWS // 2), ROWS // 2),
            [zhalf_in.at[kind, side]],
            ROWS // 2,
        )
        scatter(event + 2, chunk(zz, yy, c), zfull_in.at[kind, side], (down, up)[side])

    def wait_fulls(kind):
        for side in range(2):
            scattered(18 + 4 * kind + side, zfull_in.at[kind, side])
        return [zfull_in.at[kind, side] for side in range(2)]

    def send_y(j):
        scatter(28 + j, chunk(zs[j], yap, c), y_in.at[j], device(z, ya, c, x))

    def take_y(j):
        scattered(28 + j, y_in.at[j])
        add(chunk(zs[j], yp, c), [y_in.at[j]])

    gradient(3, True)
    cores(3, 3)
    send_y(3)
    cores(3, 2)
    send_halves(1)
    gradient(3, False)
    cores(3, 0)
    send_halves(0)
    gradient(1, True)
    cores(1, 3)
    send_y(1)
    cores(3, 1)
    gradient(2, True)
    cores(2, 3)
    send_y(2)
    take_y(3)
    send_halves(2)
    cores(1, 2)
    send_full(1, 1)
    cores(2, 2)
    send_full(1, 0)
    gradient(1, False)
    cores(1, 0)
    send_full(0, 1)
    gradient(2, False)
    cores(2, 0)
    send_full(0, 0)
    gradient(0, True)
    cores(0, 3)
    send_y(0)
    gradient(0, False)
    cores(1, 1)
    cores(2, 1)
    cores(0, 2)
    take_y(1)
    send_full(2, 1)
    take_y(2)
    send_full(2, 0)
    add(chunk(z, ya, c), wait_fulls(1))
    scatter(32, chunk(z, ya, c), y_in.at[4], device(z, ya, c, x))
    cores(0, 1)
    cores(0, 0)
    take_y(0)
    add(chunk(z, yp, c), wait_fulls(2))
    scatter(33, chunk(z, yp, c), pair_in, device(z, yp, c, x))
    terms = wait_fulls(0)
    scattered(32, y_in.at[4])
    terms = terms + [y_in.at[4]]

    def finish(i, carry):
        rows = span(i, 48)
        value = own[rows, :].astype(f32)
        for term in terms:
            value = value + term[rows, :].astype(f32)
        grad_out[rows, span(half, COLS)] = value
        return carry

    lax.fori_loop(0, ROWS // 48, finish, 0)
    scattered(33, pair_in)
    grad_out[:, span(1 - half, COLS)] = pair_in[...].astype(f32)
    for copy in sends:
        copy.wait_send()


def step(row_count, patches, group, offset, gain, embed, readout, target, master):
    vmem = pl.BlockSpec(memory_space=pltpu.VMEM)
    smem = pl.BlockSpec(memory_space=pltpu.SMEM)
    hbm = pl.BlockSpec(memory_space=pl.ANY)
    dma = pltpu.SemaphoreType.DMA
    return pl.pallas_call(
        kernel,
        out_shape=(
            jax.ShapeDtypeStruct((640, 128), bf16),
            jax.ShapeDtypeStruct((ROWS, 2 * COLS), f32),
        ),
        in_specs=[smem, vmem, vmem, vmem, vmem, hbm, hbm, hbm, hbm],
        out_specs=(vmem, vmem),
        scratch_shapes=[
            pltpu.VMEM((128, WIDTH), bf16),
            pltpu.VMEM((COLS, 128), bf16),
            pltpu.VMEM((640, 128), bf16),
            pltpu.VMEM((ROWS, COLS), f32),
            pltpu.VMEM((ROWS, COLS), f32),
            pltpu.VMEM((ROWS, COLS), bf16),
            pltpu.VMEM((8, COLS, COLS), bf16),
            pltpu.VMEM((8, TOKENS, COLS), bf16),
            pltpu.VMEM((TOKENS, COLS), f32),
            pltpu.VMEM((TOKENS, COLS), bf16),
            pltpu.VMEM((TOKENS, 128), f32),
            pltpu.VMEM((8, 1, COLS), f32),
            pltpu.VMEM((512, 512), bf16),
            pltpu.VMEM((512, 256), bf16),
            pltpu.VMEM((512, 256), bf16),
            pltpu.VMEM((512, 256), bf16),
            pltpu.VMEM((SLOTS, 256), bf16),
            pltpu.VMEM((TOKENS, 128), bf16),
            pltpu.VMEM((8, BLOCK, 128), bf16),
            pltpu.VMEM((8, BLOCK, 128), bf16),
            pltpu.VMEM((BLOCK, 128), f32),
            pltpu.VMEM((BLOCK, 128), bf16),
            pltpu.VMEM((8, BLOCK, 128), bf16),
            pltpu.VMEM((8, 2 * ROWS, COLS), bf16),
            pltpu.VMEM((3, 2, ROWS // 2, COLS), bf16),
            pltpu.VMEM((3, 2, ROWS, COLS), bf16),
            pltpu.VMEM((5, ROWS, COLS), bf16),
            pltpu.VMEM((ROWS, COLS), bf16),
            dma((5,)),
            dma((16,)),
            dma((16,)),
            dma((8,)),
            dma((8,)),
            dma((8,)),
            dma((8,)),
            dma((34,)),
            dma((34,)),
            dma((8,)),
            dma((8,)),
            dma((8,)),
            dma((8,)),
            dma((34,)),
            dma((34,)),
        ],
        compiler_params=pltpu.CompilerParams(
            collective_id=0, has_side_effects=True, vmem_limit_bytes=56 * 1024 * 1024
        ),
        name="train_step",
    )(row_count, patches, group, offset, gain, embed, readout, target, master)


def shards(
    patches,
    row_count,
    target_group,
    target_offset,
    embed,
    norm_gain,
    readout,
    target,
    master,
    moment1,
    moment2,
):
    prediction, gradient = step(
        row_count,
        patches,
        target_group.reshape(3, 128),
        target_offset.reshape(3, 128),
        norm_gain.reshape(48, 128),
        embed,
        readout,
        target,
        master,
    )
    moment1_new = beta_one * moment1 + (1.0 - beta_one) * gradient
    moment2_new = beta_two * moment2 + (1.0 - beta_two) * gradient * gradient
    first_fix = moment1_new / (1.0 - beta_one**step_count)
    second_fix = moment2_new / (1.0 - beta_two**step_count)
    master_new = master - learn_rate * (
        first_fix / (jnp.sqrt(second_fix) + adam_epsilon) + decay_rate * master
    )
    return (
        prediction.astype(f32),
        master_new,
        moment1_new,
        moment2_new,
        master_new.astype(bf16),
    )


def solution(mesh):
    placed = (
        P(("dp", "mp"), None),
        P(("dp", "mp")),
        P(("dp", "mp")),
        P(("dp", "mp")),
        P(),
        P(),
        P("mp", None),
        P("dp", None),
        P("dp", "mp"),
        P("dp", "mp"),
        P("dp", "mp"),
    )
    return jax.shard_map(
        shards,
        mesh=mesh,
        in_specs=placed,
        out_specs=(P("dp", None), P("dp", "mp"), P("dp", "mp"), P("dp", "mp"), P("dp", "mp")),
        check_vma=False,
    )
```

profile of v0, /device:TPU:0, one launch (start us, length us, event | category | flops | bytes accessed | tf_op | source)
XLA Modules:
  0.0 130.6 jit_solution(18189093717139747912)
XLA Ops:
  1.3 0.0 copy-start
  1.3 0.0 copy-start.1
  1.3 124.2 %train_step.1 = (bf16[640,128]{1,0:T(8,128)(2,1)}, f32[192,1536]{1,0:T(8,128)}) custom-call(s32[1]{0:T(128)S(6)} %copy.16.row_count, bf16[384,128]{1,0:T(8,128)(2,1)} %patches.1, s32[3,128]{1,0:T(4,128)} %bitcast.4, s32[3,128]{1,0:T(4,128)} %bitcast.5, bf16[48,128]{1,0:T(8,128)(2,1)} %bitcast.3, bf16[128,6144]{1,0:T(8,128)(2,1)} %embed_hbm.1, ...), custom_call_target="tpu_custom_call" | custom-call | tf_op jit(solution)/shard_map/train_step/pallas_call | solution.py:641
  125.5 0.0 copy-done
  125.5 0.0 copy-done.1
  125.5 0.0 copy-start.2
  125.5 4.3 %fusion.1 = (bf16[192,1536]{1,0:T(8,128)(2,1)}, f32[192,1536]{1,0:T(8,128)}, f32[192,1536]{1,0:T(8,128)}, f32[192,1536]{1,0:T(8,128)}) fusion(f32[192,1536]{1,0:T(8,128)S(1)} %copy-done, f32[192,1536]{1,0:T(8,128)} %get-tuple-element.8, f32[192,1536]{1,0:T(8,128)S(1)} %copy-done.1, f32[192,1536]{1,0:T(8,128)} %param.21), kind=kLoop, calls=%fused_computation.4 | loop fusion | flops 4718592 | bytes 8847360 | tf_op jit(solution)/shard_map/convert_element_type | solution.py:737
  129.8 0.0 copy-done.2
  129.8 0.7 convert_element_type.6
Async XLA Ops:
  1.3 124.2 %copy-start = (f32[192,1536]{1,0:T(8,128)S(1)}, f32[192,1536]{1,0:T(8,128)}, u32[]{:S(2)}) copy-start(f32[192,1536]{1,0:T(8,128)} %master_hbm.1) | copy-start | bytes 3538948
  1.3 124.2 %copy-start.1 = (f32[192,1536]{1,0:T(8,128)S(1)}, f32[192,1536]{1,0:T(8,128)}, u32[]{:S(2)}) copy-start(f32[192,1536]{1,0:T(8,128)} %param.20) | copy-start | bytes 3538948
  125.5 4.3 %copy-start.2 = (bf16[640,128]{1,0:T(8,128)(2,1)S(1)}, bf16[640,128]{1,0:T(8,128)(2,1)}, u32[]{:S(2)}) copy-start(bf16[640,128]{1,0:T(8,128)(2,1)} %get-tuple-element.7) | copy-start | bytes 491524
where the time goes:
time: 131 us
  Pallas kernels  124 us (95%)
  other arithmetic  5.03 us (4%)
  between operations  1.33 us (1%)
    pallas_call x1, Pallas kernels, step(): pl.pallas_call(kernel, out_shape=(jax.ShapeDtypeStruct((640, 128), bf16),...  124 us
    convert_element_type x1, other arithmetic, shards(): master_new.astype(bf16)  4.28 us

commit v1 on v0

--- a/solution.py
+++ b/solution.py
@@ -328,8 +328,9 @@
             wait_y(0)
             relay(0, 3)
 
-        @pl.when(j == 6)
-        def _():
+        @pl.when(j == 5)
+        def _():
+            along_y(3)
             wait_full(6, ya)
             halves_z(6, ya)
             relay(1, 2)
@@ -365,7 +366,6 @@
         @pl.when(i == 3)
         def _():
             wait_y(1)
-            along_y(3)
             relay(1, 3)
             wait_halves(2, y)
             relay(3, 0)
@@ -590,23 +590,23 @@
     send_full(1, 1)
     cores(2, 2)
     send_full(1, 0)
+    gradient(0, True)
+    cores(0, 3)
+    send_y(0)
     gradient(1, False)
     cores(1, 0)
     send_full(0, 1)
     gradient(2, False)
     cores(2, 0)
     send_full(0, 0)
-    gradient(0, True)
-    cores(0, 3)
-    send_y(0)
-    gradient(0, False)
     cores(1, 1)
-    cores(2, 1)
-    cores(0, 2)
     take_y(1)
     send_full(2, 1)
+    cores(2, 1)
     take_y(2)
     send_full(2, 0)
+    gradient(0, False)
+    cores(0, 2)
     add(chunk(z, ya, c), wait_fulls(1))
     scatter(32, chunk(z, ya, c), y_in.at[4], device(z, ya, c, x))
     cores(0, 1)

time: 131 us -> 135 us (1.031)
  Pallas kernels: 124 us -> 128 us
    pallas_call x1, Pallas kernels: 124 us -> 128 us  [step(): pl.pallas_call(kernel, out_shape=(jax.ShapeDtypeStruct((640, 128), bf16),...]
where the time goes in v1:
time: 135 us; the launch traced here: 134 us
  Pallas kernels  128 us (95%)
  other arithmetic  5.03 us (4%)
    pallas_call x1, Pallas kernels, step(): pl.pallas_call(kernel, out_shape=(jax.ShapeDtypeStruct((640, 128), bf16),...  128 us
    convert_element_type x1, other arithmetic, shards(): master_new.astype(bf16)  4.28 us

profile of v1, /device:TPU:0, one launch (start us, length us, event | category | flops | bytes accessed | tf_op | source)
XLA Modules:
  0.0 134.1 jit_solution(8620398416210974633)
XLA Ops:
  1.3 0.0 copy-start
  1.3 0.0 copy-start.1
  1.3 127.7 %train_step.1 = (bf16[640,128]{1,0:T(8,128)(2,1)}, f32[192,1536]{1,0:T(8,128)}) custom-call(s32[1]{0:T(128)S(6)} %copy.16.row_count, bf16[384,128]{1,0:T(8,128)(2,1)} %patches.1, s32[3,128]{1,0:T(4,128)} %bitcast.4, s32[3,128]{1,0:T(4,128)} %bitcast.5, bf16[48,128]{1,0:T(8,128)(2,1)} %bitcast.3, bf16[128,6144]{1,0:T(8,128)(2,1)} %embed_hbm.1, ...), custom_call_target="tpu_custom_call" | custom-call | tf_op jit(solution)/shard_map/train_step/pallas_call | solution.py:641
  129.0 0.0 copy-done
  129.0 0.0 copy-done.1
  129.0 0.0 copy-start.2
  129.0 4.3 %fusion.1 = (bf16[192,1536]{1,0:T(8,128)(2,1)}, f32[192,1536]{1,0:T(8,128)}, f32[192,1536]{1,0:T(8,128)}, f32[192,1536]{1,0:T(8,128)}) fusion(f32[192,1536]{1,0:T(8,128)S(1)} %copy-done, f32[192,1536]{1,0:T(8,128)} %get-tuple-element.8, f32[192,1536]{1,0:T(8,128)S(1)} %copy-done.1, f32[192,1536]{1,0:T(8,128)} %param.21), kind=kLoop, calls=%fused_computation.4 | loop fusion | flops 4718592 | bytes 8847360 | tf_op jit(solution)/shard_map/convert_element_type | solution.py:737
  133.3 0.0 copy-done.2
  133.3 0.7 convert_element_type.6
Async XLA Ops:
  1.3 127.7 %copy-start = (f32[192,1536]{1,0:T(8,128)S(1)}, f32[192,1536]{1,0:T(8,128)}, u32[]{:S(2)}) copy-start(f32[192,1536]{1,0:T(8,128)} %master_hbm.1) | copy-start | bytes 3538948
  1.3 127.7 %copy-start.1 = (f32[192,1536]{1,0:T(8,128)S(1)}, f32[192,1536]{1,0:T(8,128)}, u32[]{:S(2)}) copy-start(f32[192,1536]{1,0:T(8,128)} %param.20) | copy-start | bytes 3538948
  129.0 4.3 %copy-start.2 = (bf16[640,128]{1,0:T(8,128)(2,1)S(1)}, bf16[640,128]{1,0:T(8,128)(2,1)}, u32[]{:S(2)}) copy-start(bf16[640,128]{1,0:T(8,128)(2,1)} %get-tuple-element.7) | copy-start | bytes 491524

commit v2 on v0

--- a/solution.py
+++ b/solution.py
@@ -328,8 +328,9 @@
             wait_y(0)
             relay(0, 3)
 
-        @pl.when(j == 6)
-        def _():
+        @pl.when(j == 5)
+        def _():
+            along_y(3)
             wait_full(6, ya)
             halves_z(6, ya)
             relay(1, 2)
@@ -365,7 +366,6 @@
         @pl.when(i == 3)
         def _():
             wait_y(1)
-            along_y(3)
             relay(1, 3)
             wait_halves(2, y)
             relay(3, 0)

time: 131 us -> 132 us (level)
  Pallas kernels: 124 us -> 126 us
    pallas_call x1, Pallas kernels: 124 us -> 126 us  [step(): pl.pallas_call(kernel, out_shape=(jax.ShapeDtypeStruct((640, 128), bf16),...]
where the time goes in v2:
time: 132 us
  Pallas kernels  126 us (95%)
  other arithmetic  5.03 us (4%)
  between operations  1.33 us (1%)
    pallas_call x1, Pallas kernels, step(): pl.pallas_call(kernel, out_shape=(jax.ShapeDtypeStruct((640, 128), bf16),...  126 us
    convert_element_type x1, other arithmetic, shards(): master_new.astype(bf16)  4.28 us

profile of v2, /device:TPU:0, one launch (start us, length us, event | category | flops | bytes accessed | tf_op | source)
XLA Modules:
  0.0 132.2 jit_solution(16348089016844385613)
XLA Ops:
  1.3 0.0 copy-start
  1.3 0.0 copy-start.1
  1.3 125.8 %train_step.1 = (bf16[640,128]{1,0:T(8,128)(2,1)}, f32[192,1536]{1,0:T(8,128)}) custom-call(s32[1]{0:T(128)S(6)} %copy.16.row_count, bf16[384,128]{1,0:T(8,128)(2,1)} %patches.1, s32[3,128]{1,0:T(4,128)} %bitcast.4, s32[3,128]{1,0:T(4,128)} %bitcast.5, bf16[48,128]{1,0:T(8,128)(2,1)} %bitcast.3, bf16[128,6144]{1,0:T(8,128)(2,1)} %embed_hbm.1, ...), custom_call_target="tpu_custom_call" | custom-call | tf_op jit(solution)/shard_map/train_step/pallas_call | solution.py:641
  127.1 0.0 copy-done
  127.1 0.0 copy-done.1
  127.1 0.0 copy-start.2
  127.1 4.3 %fusion.1 = (bf16[192,1536]{1,0:T(8,128)(2,1)}, f32[192,1536]{1,0:T(8,128)}, f32[192,1536]{1,0:T(8,128)}, f32[192,1536]{1,0:T(8,128)}) fusion(f32[192,1536]{1,0:T(8,128)S(1)} %copy-done, f32[192,1536]{1,0:T(8,128)} %get-tuple-element.8, f32[192,1536]{1,0:T(8,128)S(1)} %copy-done.1, f32[192,1536]{1,0:T(8,128)} %param.21), kind=kLoop, calls=%fused_computation.4 | loop fusion | flops 4718592 | bytes 8847360 | tf_op jit(solution)/shard_map/convert_element_type | solution.py:737
  131.4 0.0 copy-done.2
  131.4 0.7 convert_element_type.6
Async XLA Ops:
  1.3 125.8 %copy-start = (f32[192,1536]{1,0:T(8,128)S(1)}, f32[192,1536]{1,0:T(8,128)}, u32[]{:S(2)}) copy-start(f32[192,1536]{1,0:T(8,128)} %master_hbm.1) | copy-start | bytes 3538948
  1.3 125.8 %copy-start.1 = (f32[192,1536]{1,0:T(8,128)S(1)}, f32[192,1536]{1,0:T(8,128)}, u32[]{:S(2)}) copy-start(f32[192,1536]{1,0:T(8,128)} %param.20) | copy-start | bytes 3538948
  127.1 4.3 %copy-start.2 = (bf16[640,128]{1,0:T(8,128)(2,1)S(1)}, bf16[640,128]{1,0:T(8,128)(2,1)}, u32[]{:S(2)}) copy-start(bf16[640,128]{1,0:T(8,128)(2,1)} %get-tuple-element.7) | copy-start | bytes 491524
